TPU v7x, 512 devices: a whole 4x8x8 slice. The times are simulated.
512 devices in a mesh: grp: 16 (over z, core), ctx: 32 (over y, x).
Axes of the slice: x: 4, y: 8, z: 8, core: 2. Of those that a mesh axis runs over, the one named last changes fastest.
Arguments:
- q_resp: bfloat16 [32768, 4096], P(('grp', 'ctx')), parts along dimension 0, may hold values from -6 to 6
- k_resp: bfloat16 [32768, 512], P(('grp', 'ctx')), parts along dimension 0, may hold values from -6 to 6
- v_resp: bfloat16 [32768, 512], P(('grp', 'ctx')), parts along dimension 0, may hold values from -6 to 6
- k_prompt: bfloat16 [32768, 512], P(('grp', 'ctx')), parts along dimension 0, may hold values from -6 to 6
- v_prompt: bfloat16 [32768, 512], P(('grp', 'ctx')), parts along dimension 0, may hold values from -6 to 6
- d_out: bfloat16 [32768, 4096], P(('grp', 'ctx')), parts along dimension 0, may hold values from -6 to 6
- owner: int32 [512], P('grp'), parts along dimension 0, may hold values from 0 to 31, each once
- lengths: int32 [512], P('grp'), parts along dimension 0, may hold values from 16 to 64, as said below
- visible: int32 [512], P('grp'), parts along dimension 0, may hold values from 1024 to 2048, as said below
Outputs:
- out: bfloat16 [32768, 4096], P(('grp', 'ctx')), parts along dimension 0
- dq: bfloat16 [32768, 4096], P(('grp', 'ctx')), parts along dimension 0
- dk_prompt: bfloat16 [32768, 512], P(('grp', 'ctx')), parts along dimension 0
- dv_prompt: bfloat16 [32768, 512], P(('grp', 'ctx')), parts along dimension 0
- dk_resp: bfloat16 [32768, 512], P(('grp', 'ctx')), parts along dimension 0
- dv_resp: bfloat16 [32768, 512], P(('grp', 'ctx')), parts along dimension 0
There are 16 independent parts, one for each index of `grp`. A program takes and returns all parts, laid end to end along the dimension named above; each array names one. Nothing has to cross between parts.
Inputs may be any that keep to these rules, and one draw needn't show every extreme that they name: `lengths`: some response fills all 64 positions of its window. `visible`: some response attends to the whole prompt.
All inputs are finite; a program needn't handle non-finite values.
Results may differ from a plain program's by a relative error of at most 0.022.
Values may be sent and summed in bfloat16 or wider, within the bound.
A program may use at most 128 MiB of HBM per device.

v0:
```python
import math

import jax
import jax.numpy as jnp
from jax import lax
from jax.sharding import PartitionSpec as P

H = 32
G = 4
HD = 128


NEG_FILL = -1e30


def slot_tables(owner, lengths, visible, shards):
    matching = owner[None, :] == jnp.arange(shards, dtype=jnp.int32)[:, None]
    slot_length = jnp.sum(jnp.where(matching, lengths[None, :], 0), axis=1)
    slot_visible = jnp.sum(jnp.where(matching, visible[None, :], 0), axis=1)
    return (slot_length, slot_visible)


def head_block(matrix, kv_group):
    group_width = H // G * HD
    return matrix[:, kv_group * group_width : (kv_group + 1) * group_width].reshape(
        matrix.shape[0], H // G, HD
    )


def key_block(matrix, kv_group):
    return matrix[:, kv_group * HD : (kv_group + 1) * HD]


def forward_part(queries, keys, values, allowed, score_scale):
    max_parts, total_parts, out_parts = ([], [], [])
    for kv_group in range(G):
        scores = (
            jnp.einsum(
                "qrd,kd->qrk",
                head_block(queries, kv_group),
                key_block(keys, kv_group),
                preferred_element_type=jnp.float32,
            )
            * score_scale
        )
        block_max = jnp.max(jnp.where(allowed, scores, NEG_FILL), axis=-1)
        weights = jnp.where(allowed, jnp.exp(scores - block_max[..., None]), 0.0)
        group_out = jnp.einsum(
            "qrk,kd->qrd",
            weights.astype(jnp.bfloat16),
            key_block(values, kv_group),
            preferred_element_type=jnp.float32,
        )
        max_parts.append(block_max)
        total_parts.append(jnp.sum(weights, axis=-1))
        out_parts.append(group_out)
    return (
        jnp.concatenate(max_parts, axis=1),
        jnp.concatenate(total_parts, axis=1),
        jnp.concatenate(out_parts, axis=1),
    )


def backward_part(queries, grads, keys, values, allowed, norms, deltas, score_scale):
    heads_per = H // G
    query_parts, key_parts, value_parts = ([], [], [])
    for kv_group in range(G):
        group_queries = head_block(queries, kv_group)
        group_grads = head_block(grads, kv_group)
        group_keys = key_block(keys, kv_group)
        group_values = key_block(values, kv_group)
        group_norm = norms[:, kv_group * heads_per : (kv_group + 1) * heads_per]
        group_delta = deltas[:, kv_group * heads_per : (kv_group + 1) * heads_per]
        scores = (
            jnp.einsum("qrd,kd->qrk", group_queries, group_keys, preferred_element_type=jnp.float32)
            * score_scale
        )
        probability = jnp.where(allowed, jnp.exp(scores - group_norm[..., None]), 0.0)
        value_parts.append(
            jnp.einsum(
                "qrk,qrd->kd",
                probability.astype(jnp.bfloat16),
                group_grads,
                preferred_element_type=jnp.float32,
            )
        )
        prob_grad = jnp.einsum(
            "qrd,kd->qrk", group_grads, group_values, preferred_element_type=jnp.float32
        )
        score_grad = (probability * (prob_grad - group_delta[..., None])).astype(jnp.bfloat16)
        query_grad = (
            jnp.einsum("qrk,kd->qrd", score_grad, group_keys, preferred_element_type=jnp.float32)
            * score_scale
        )
        query_parts.append(query_grad.reshape(query_grad.shape[0], heads_per * HD))
        key_parts.append(
            jnp.einsum("qrk,qrd->kd", score_grad, group_queries, preferred_element_type=jnp.float32)
            * score_scale
        )
    return (
        jnp.concatenate(query_parts, axis=1),
        jnp.concatenate(key_parts, axis=1),
        jnp.concatenate(value_parts, axis=1),
    )


def body(q_resp, k_resp, v_resp, k_prompt, v_prompt, d_out, owner, lengths, visible):
    shards = lax.axis_size("ctx")
    my_index = lax.axis_index("ctx")
    window = q_resp.shape[0]
    score_scale = 1.0 / math.sqrt(HD)
    slot_length, slot_visible = slot_tables(owner, lengths, visible, shards)
    slot_ids = jnp.arange(shards, dtype=jnp.int32)
    my_length = jnp.sum(jnp.where(slot_ids == my_index, slot_length, 0))
    my_visible = jnp.sum(jnp.where(slot_ids == my_index, slot_visible, 0))
    all_keys, all_values = (
        lax.all_gather(k_prompt, "ctx", axis=0, tiled=True),
        lax.all_gather(v_prompt, "ctx", axis=0, tiled=True),
    )
    prompt_total = all_keys.shape[0]
    prompt_allowed = (jnp.arange(prompt_total, dtype=jnp.int32) < my_visible)[None, None, :]
    key_pos = jnp.arange(window, dtype=jnp.int32)
    window_allowed = (
        (key_pos[None, :] >= window - my_length) & (key_pos[None, :] <= key_pos[:, None])
    )[:, None, :]
    prompt_max, prompt_sum, prompt_out = forward_part(
        q_resp, all_keys, all_values, prompt_allowed, score_scale
    )
    window_max, window_sum, window_out = forward_part(
        q_resp, k_resp, v_resp, window_allowed, score_scale
    )
    overall = jnp.maximum(prompt_max, window_max)
    prompt_factor = jnp.exp(prompt_max - overall)
    window_factor = jnp.exp(window_max - overall)
    denominator = prompt_factor * prompt_sum + window_factor * window_sum
    attended = (
        prompt_factor[..., None] * prompt_out + window_factor[..., None] * window_out
    ) / denominator[..., None]
    log_norm = overall + jnp.log(denominator)
    row_delta = jnp.sum(d_out.astype(jnp.float32).reshape(window, H, HD) * attended, axis=-1)
    out = attended.reshape(window, H * HD).astype(jnp.bfloat16)
    prompt_qgrad, prompt_kgrad, prompt_vgrad = backward_part(
        q_resp, d_out, all_keys, all_values, prompt_allowed, log_norm, row_delta, score_scale
    )
    window_qgrad, window_kgrad, window_vgrad = backward_part(
        q_resp, d_out, k_resp, v_resp, window_allowed, log_norm, row_delta, score_scale
    )
    grad_terms = jnp.concatenate((prompt_kgrad, prompt_vgrad), axis=1)
    summed = lax.psum_scatter(
        grad_terms.astype(jnp.bfloat16), "ctx", scatter_dimension=0, tiled=True
    ).astype(jnp.float32)
    dk_prompt = summed[:, : G * HD].astype(jnp.bfloat16)
    dv_prompt = summed[:, G * HD :].astype(jnp.bfloat16)
    dq = (prompt_qgrad + window_qgrad).astype(jnp.bfloat16)
    return (
        out,
        dq,
        dk_prompt,
        dv_prompt,
        window_kgrad.astype(jnp.bfloat16),
        window_vgrad.astype(jnp.bfloat16),
    )


def solution(mesh):
    in_specs = (
        P(("grp", "ctx"), None),
        P(("grp", "ctx"), None),
        P(("grp", "ctx"), None),
        P(("grp", "ctx"), None),
        P(("grp", "ctx"), None),
        P(("grp", "ctx"), None),
        P("grp"),
        P("grp"),
        P("grp"),
    )
    out_specs = (
        P(("grp", "ctx"), None),
        P(("grp", "ctx"), None),
        P(("grp", "ctx"), None),
        P(("grp", "ctx"), None),
        P(("grp", "ctx"), None),
        P(("grp", "ctx"), None),
    )
    return jax.shard_map(body, mesh=mesh, in_specs=in_specs, out_specs=out_specs, check_vma=False)
```

profile of v0, /device:TPU:16, one launch (start us, length us, event | category | flops | bytes accessed | tf_op | source)
XLA Modules:
  0.0 451.3 jit_solution(13690278816275946745)
XLA Ops:
  8.7 1.1 slice_bitcast_fusion.27
  9.8 1.1 convert_bitcast_fusion
  14.4 1.2 slice_bitcast_fusion.28
  20.9 1.8 fusion.87
  23.0 1.1 fusion.89
  25.4 73.1 %all-gather.3.cloned.1.call-done = bf16[2048,512]{1,0:T(8,128)(2,1)} async-done(((bf16[64,512]{1,0:T(8,128)(2,1)}), bf16[2048,512]{1,0:T(8,128)(2,1)}) %all-gather.3.cloned.1.call-update) | async-done | bytes 2097168 | tf_op jit(solution)/shard_map/all_gather | solution.py:117
  98.5 1.9 fusion.85
  102.0 2.7 fusion
  105.0 3.0 fusion.2
  109.4 73.0 %all-gather.5.cloned.1.call-done = bf16[2048,512]{1,0:T(8,128)(2,1)} async-done(((bf16[64,512]{1,0:T(8,128)(2,1)}), bf16[2048,512]{1,0:T(8,128)(2,1)}) %all-gather.5.cloned.1.call-update) | async-done | bytes 2097168 | tf_op jit(solution)/shard_map/all_gather | solution.py:118
  182.4 3.2 fusion.50
  187.5 1.4 copy-done.1
  189.7 1.4 copy-done.15
  192.0 1.9 multiply_reduce_fusion
  194.1 1.3 multiply_convert_fusion.3
  195.4 1.5 fusion.17
  196.9 1.3 multiply_convert_fusion.2
  198.3 1.6 fusion.19
  199.8 1.3 multiply_convert_fusion.1
  201.1 1.3 fusion.21
  202.4 1.3 multiply_convert_fusion
  203.7 1.5 fusion.23
  205.2 1.8 fusion.25
  207.0 1.8 fusion.27
  208.8 1.8 fusion.29
  210.6 1.8 fusion.31
  212.4 6.4 %copy.85 = bf16[2048,1024]{1,0:T(8,128)(2,1)} copy(bf16[2048,1024]{0,1:T(8,128)(2,1)} %fusion.31) | data formatting | bytes 8388608
  218.9 2.2 copy.116
  221.1 1.2 fusion.64
  222.5 1.2 fusion.67
  231.8 211.4 %reduce-scatter.4.cloned.1.call-done = bf16[64,1024]{1,0:T(8,128)(2,1)} async-done(((bf16[2048,1024]{1,0:T(8,128)(2,1)}), bf16[64,1024]{1,0:T(8,128)(2,1)}) %reduce-scatter.4.cloned.1.call-update) | async-done | bytes 131088
  443.2 1.5 fusion.198
  (179 shorter events, 26.2 us)
Async XLA Ops:
  7.2 8.5 %copy-start.20 = (bf16[64,512]{1,0:T(8,128)(2,1)S(1)}, bf16[64,512]{1,0:T(8,128)(2,1)}, u32[]{:S(2)}) copy-start(bf16[64,512]{1,0:T(8,128)(2,1)} %param.10) | copy-start | bytes 196612
  7.2 91.3 %all-gather.3.cloned.1.call-start = ((), (), s32[]{:S(2)}) async-start(), calls=%async_computation.1 | async-start | bytes 2162688 | tf_op jit(solution)/shard_map/all_gather | solution.py:117
  7.9 174.5 %all-gather.5.cloned.1.call-start = ((), (), s32[]{:S(2)}) async-start(), calls=%async_computation.2 | async-start | bytes 2162688 | tf_op jit(solution)/shard_map/all_gather | solution.py:118
  8.7 434.6 %reduce-scatter.4.cloned.1.call-start = ((), (), s32[]{:S(2)}) async-start(), calls=%async_computation.3 | async-start | bytes 4325376
  14.4 8.4 %copy-start.43 = (bf16[64,512]{1,0:T(8,128)(2,1)S(1)}, bf16[64,512]{1,0:T(8,128)(2,1)}, u32[]{:S(2)}) copy-start(bf16[64,512]{1,0:T(8,128)(2,1)} %param.11) | copy-start | bytes 196612
  15.6 8.5 %copy-start.16 = (bf16[8,8,8,128]{3,2,1,0:T(8,128)(2,1)}, bf16[8,8,8,128]{3,2,1,0:T(8,128)(2,1)S(1)}, u32[]{:S(2)}) copy-start(bf16[8,8,8,128]{3,2,1,0:T(8,128)(2,1)S(1)} %copy.90) | copy-start | bytes 393220
  100.4 4.5 %copy-start.2 = (f32[64,8,2048]{2,1,0:T(8,128)}, f32[64,8,2048]{2,1,0:T(8,128)S(1)}, u32[]{:S(2)}) copy-start(f32[64,8,2048]{2,1,0:T(8,128)S(1)} %fusion.85) | copy-start | bytes 12582916
  101.1 3.8 copy-start
  104.7 3.2 copy-start.14
  104.8 3.2 copy-start.24
  104.8 3.2 copy-start.26
  104.8 3.2 copy-start.28
  105.0 3.0 copy-start.39
  105.0 3.1 copy-start.40
  105.0 3.1 copy-start.41
  105.0 77.4 %copy-start.23 = (f32[64,8]{1,0:T(8,128)S(1)}, f32[64,8]{1,0:T(8,128)}, u32[]{:S(2)}) copy-start(f32[64,8]{1,0:T(8,128)} %copy-done.22) | copy-start | bytes 6148
  108.0 77.6 %copy-start.29 = (f32[64,8]{1,0:T(8,128)S(1)}, f32[64,8]{1,0:T(8,128)}, u32[]{:S(2)}) copy-start(f32[64,8]{1,0:T(8,128)} %copy-done.28) | copy-start | bytes 6148
  182.4 3.6 copy-start.3
  182.4 4.3 copy-start.59
  194.1 5.7 %copy-start.55 = (f32[64,8]{1,0:T(8,128)}, f32[64,8]{1,0:T(8,128)S(1)}, u32[]{:S(2)}) copy-start(f32[64,8]{1,0:T(8,128)S(1)} %get-tuple-element.65) | copy-start | bytes 6148
  194.1 8.3 %copy-start.57 = (f32[64,8]{1,0:T(8,128)}, f32[64,8]{1,0:T(8,128)S(1)}, u32[]{:S(2)}) copy-start(f32[64,8]{1,0:T(8,128)S(1)} %get-tuple-element.64) | copy-start | bytes 6148
  203.7 3.3 copy-start.4
  218.8 5.1 %copy-start.33 = (bf16[8,8,8,128]{3,2,1,0:T(8,128)(2,1)S(1)}, bf16[8,8,8,128]{3,2,1,0:T(8,128)(2,1)}, u32[]{:S(2)}) copy-start(bf16[8,8,8,128]{3,2,1,0:T(8,128)(2,1)} %copy.99) | copy-start | bytes 393220
  218.8 5.1 %copy-start.44 = (bf16[64,512]{1,0:T(8,128)(2,1)S(1)}, bf16[64,512]{1,0:T(8,128)(2,1)}, u32[]{:S(2)}) copy-start(bf16[64,512]{1,0:T(8,128)(2,1)} %param.11) | copy-start | bytes 196612
  218.8 5.1 %copy-start.48 = (f32[64,8]{1,0:T(8,128)S(1)}, f32[64,8]{1,0:T(8,128)}, u32[]{:S(2)}) copy-start(f32[64,8]{1,0:T(8,128)} %get-tuple-element.61) | copy-start | bytes 6148
  218.8 5.1 %copy-start.56 = (f32[64,8]{1,0:T(8,128)S(1)}, f32[64,8]{1,0:T(8,128)}, u32[]{:S(2)}) copy-start(f32[64,8]{1,0:T(8,128)} %copy-done.55) | copy-start | bytes 6148
  218.9 5.5 %copy-start.31 = (bf16[8,8,8,128]{3,2,1,0:T(8,128)(2,1)S(1)}, bf16[8,8,8,128]{3,2,1,0:T(8,128)(2,1)}, u32[]{:S(2)}) copy-start(bf16[8,8,8,128]{3,2,1,0:T(8,128)(2,1)} %copy.97) | copy-start | bytes 393220
  218.9 5.5 %copy-start.46 = (f32[64,8]{1,0:T(8,128)S(1)}, f32[64,8]{1,0:T(8,128)}, u32[]{:S(2)}) copy-start(f32[64,8]{1,0:T(8,128)} %get-tuple-element.62) | copy-start | bytes 6148
  218.9 5.5 %copy-start.54 = (f32[64,8]{1,0:T(8,128)S(1)}, f32[64,8]{1,0:T(8,128)}, u32[]{:S(2)}) copy-start(f32[64,8]{1,0:T(8,128)} %copy-done.53) | copy-start | bytes 6148
  218.9 5.8 %copy-start.18 = (bf16[8,8,8,128]{3,2,1,0:T(8,128)(2,1)S(1)}, bf16[8,8,8,128]{3,2,1,0:T(8,128)(2,1)}, u32[]{:S(2)}) copy-start(bf16[8,8,8,128]{3,2,1,0:T(8,128)(2,1)} %copy-done.16) | copy-start | bytes 393220
  221.1 3.8 copy-start.37
  221.1 3.8 copy-start.52
  (31 other events, 79.3 us)
Sparse Core Ops, SparseCore 0:
  11.2 87.2 all-gather.2
  101.6 80.7 all-gather.4
  218.9 224.2 reduce-scatter.3
where the time goes:
time: 452 us; the launch traced here: 451 us
  waiting for transfers between devices  359 us (79%)
  matrix products  44 us (10%)
  local copies, waits for them, and re-layouts  20.8 us (5%)
  between operations  15.3 us (3%)
  other arithmetic  12.3 us (3%)
    unnamed x4, waiting for transfers between devices  213 us
    all_gather x1, waiting for transfers between devices, body(): lax.all_gather(k_prompt, 'ctx', axis=0, tiled=True)  73.1 us
    all_gather x1, waiting for transfers between devices, body(): lax.all_gather(v_prompt, 'ctx', axis=0, tiled=True)  73 us
    unnamed x133, local copies, waits for them, and re-layouts  18.1 us
    dot_general x8, matrix products, forward_part(): jnp.einsum('qrd,kd->qrk', head_block(queries, kv_group), key_block(keys,...  9.33 us
  transfers between devices with their start and end apart: 3, of which 3 were waited for; matrix products, arithmetic and copies ran while one was open for 9% of the time, Pallas kernels for 0%

commit v1 on v0

v1 whole, which is shorter than its diff:
```python
import functools
import math

import jax
import jax.numpy as jnp
from jax import lax
from jax.experimental import pallas as pl
from jax.experimental.pallas import tpu as pltpu
from jax.sharding import PartitionSpec as P

H = 32
G = 4
HD = 128
HPG = H // G
GW = HPG * HD
X = 4
Y = 8
W = 64
ROWS = HPG * W
CHUNK = X * W
NEG = -1e30
SCALE = 1.0 / math.sqrt(HD)
LOG2 = SCALE * math.log2(math.e)
MESH = pl.DeviceIdType.MESH
BF = jnp.bfloat16
F32 = jnp.float32
UP, DOWN = 0, 1
PIECES = 2
PIECE = CHUNK // PIECES
OFF = (0, 1, 3, 2)
SLOT = (0, 1, 3, 2)


def dot(a, b):
    return lax.dot_general(a, b, (((1,), (0,)), ((), ())), preferred_element_type=F32)


def kernel(
    owner, lengths, visible, q, kr, vr, kp, vp, do,
    out, dq, dkp, dvp, dkr, dvr,
    slots, qb, dob, krb, vrb, kv, kt, vt, qt, dot_t, eb, wb, mb, mcur, oacc, stat,
    dqacc, dkacc, dvacc, outs, dqs, dkrs, dvrs, rs_s, rs_r, fin,
    in_ls, in_ss, in_rs, ag_ss, ag_rs, out_ls, out_ss, out_rs, rs_ss, rs_rs,
):
    c = lax.axis_index("ctx")
    y = c // X
    x = lax.rem(c, X)

    def peer(d):
        return {"ctx": y * X + lax.rem(x + d, X)}

    def ring(direction):
        return {"ctx": lax.rem(y + (1 if direction == UP else Y - 1), Y) * X + x}

    barrier = pltpu.get_barrier_semaphore()
    for device in (peer(1), peer(2), peer(3), ring(UP), ring(DOWN)):
        pl.semaphore_signal(barrier, inc=1, device_id=device, device_id_type=MESH)

    sources = ((kp, HD), (vp, HD), (kr, HD), (vr, HD), (q, GW), (do, GW))

    def landing(kind, slot):
        if kind < 2:
            return kv.at[0, slot, kind]
        return (krb, vrb, qb, dob)[kind - 2].at[slot]

    def enter(kind, d):
        ref, width = sources[kind]
        column = pl.multiple_of(lax.rem(x + d, X) * width, HD)
        return pltpu.make_async_remote_copy(
            src_ref=ref.at[:, pl.ds(column, width)],
            dst_ref=landing(kind, SLOT[X - d]),
            send_sem=in_ss.at[kind, d - 1],
            recv_sem=in_rs.at[kind, d - 1],
            device_id=peer(d),
            device_id_type=MESH,
        )

    def enter_own(kind):
        ref, width = sources[kind]
        column = pl.multiple_of(x * width, HD)
        return pltpu.make_async_copy(
            ref.at[:, pl.ds(column, width)], landing(kind, 0), in_ls.at[kind]
        )

    def entered(kind, i):
        if i == 0:
            enter_own(kind).wait()
        else:
            enter(kind, X - OFF[i]).wait_recv()

    for kind in range(6):
        enter_own(kind).start()

    for i in range(X):
        holder = y * X + lax.rem(x + OFF[i], X)

        def count(j, carry, holder=holder):
            hit = owner[j] == holder
            return (
                carry[0] + jnp.where(hit, lengths[j], 0),
                carry[1] + jnp.where(hit, visible[j], 0),
            )

        length, seen = lax.fori_loop(0, Y * X, count, (jnp.int32(0), jnp.int32(0)))
        slots[0, i] = length
        slots[1, i] = seen

    pl.semaphore_wait(barrier, 5)
    for kind in range(6):
        for d in (1, 3, 2):
            enter(kind, d).start()

    def gather(hop, direction, i):
        away = (1 - hop) % Y if direction == UP else hop - 1
        there = -hop % Y if direction == UP else hop
        src, dst = kv.at[away, i], kv.at[there, i]
        if hop == 4:
            src, dst = kv.at[away, i, direction], kv.at[there, i, direction]
        return pltpu.make_async_remote_copy(
            src_ref=src,
            dst_ref=dst,
            send_sem=ag_ss.at[hop - 1, direction, i],
            recv_sem=ag_rs.at[hop - 1, direction, i],
            device_id=ring(direction),
            device_id_type=MESH,
        )

    def spread(i):
        for kind in (0, 1):
            entered(kind, i)
        for direction in (UP, DOWN):
            gather(1, direction, i).start()

    def hop_on(hop, i):
        for direction in (UP, DOWN):
            gather(hop, direction, i).wait_recv()
            if hop < 4:
                gather(hop + 1, direction, i).start()

    def turn(a):
        kt[a] = kv[a, :, 0].reshape(CHUNK, HD).T
        vt[a, 0:HD, :] = kv[a, :, 1].reshape(CHUNK, HD).T
        vt[a, HD:, :] = jnp.ones((16, CHUNK), BF)

    def natural(ref, i):
        return jnp.concatenate([ref[i, :, n * HD : (n + 1) * HD] for n in range(HPG)], axis=0)

    def chunks_of(step):
        return (step,) if step in (0, 4) else (Y - step, step)

    def soften(i, step, scores, values_t, keep):
        top = functools.reduce(
            jnp.maximum, [jnp.max(s, axis=0, keepdims=True) for s in scores]
        )
        if step is not None:
            before = mcur[i]
            top = jnp.maximum(top, before)
        mcur[i] = top
        mb[i, 5 if step is None else step] = top
        total = None
        for s, values, ref in zip(scores, values_t, keep):
            e = jnp.exp2((s - top) * LOG2).astype(BF)
            ref[...] = e
            term = dot(values, e)
            total = term if total is None else total + term
        if step is None:
            oacc[i] = total
        else:
            oacc[i] = oacc[i] * jnp.exp2((before - top) * LOG2) + total

    def ready(i):
        for kind in (2, 3, 4):
            entered(kind, i)
        qt[i] = natural(qb, i).T
        key = lax.broadcasted_iota(jnp.int32, (W, ROWS), 0)
        query = lax.rem(lax.broadcasted_iota(jnp.int32, (W, ROWS), 1), W)
        allowed = (key >= W - slots[0, i]) & (key <= query)
        scores = jnp.where(allowed, dot(krb[i], qt[i]), NEG)
        values = jnp.concatenate([vrb[i].T, jnp.ones((16, W), BF)], axis=0)
        soften(i, None, [scores], [values], [wb.at[i]])

    def forward(i, step):
        seen = slots[1, i]
        scores, values, keep = [], [], []
        for a in chunks_of(step):
            s = dot(kv[a, :, 0].reshape(CHUNK, HD), qt[i])
            first = lax.rem(y + a, Y) * CHUNK
            key = lax.broadcasted_iota(jnp.int32, (W, 1), 0) + first
            left = jnp.concatenate([key + lax.rem(x + OFF[n], X) * W for n in range(X)], axis=0)
            scores.append(jnp.where(left < seen, s, NEG))
            values.append(vt[a])
            keep.append(eb.at[i, a])
        soften(i, step, scores, values, keep)

    targets = ((outs, out, GW), (dqs, dq, GW), (dkrs, dkr, HD), (dvrs, dvr, HD), (None, dkp, HD), (None, dvp, HD))

    def leave_source(kind, i):
        if kind >= 4:
            return fin.at[kind - 4, i]
        return targets[kind][0].at[i]

    def leave_target(kind):
        ref, width = targets[kind][1:]
        return ref.at[:, pl.ds(pl.multiple_of(x * width, HD), width)]

    def leave(kind, d):
        return pltpu.make_async_remote_copy(
            src_ref=leave_source(kind, SLOT[d]),
            dst_ref=leave_target(kind),
            send_sem=out_ss.at[kind, d - 1],
            recv_sem=out_rs.at[kind, d - 1],
            device_id=peer(d),
            device_id_type=MESH,
        )

    def leave_own(kind):
        return pltpu.make_async_copy(leave_source(kind, 0), leave_target(kind), out_ls.at[kind])

    def go(kind, i):
        if i == 0:
            leave_own(kind).start()
        else:
            leave(kind, OFF[i]).start()

    def finish(i):
        entered(5, i)
        inverse = 1.0 / oacc[i, HD : HD + 1, :]
        attended = oacc[i, 0:HD, :] * inverse
        grads_t = natural(dob, i).T
        dot_t[i] = grads_t
        stat[i, 0:1, :] = jnp.sum(grads_t.astype(F32) * attended, axis=0, keepdims=True)
        stat[i, 1:2, :] = inverse
        turned = attended.T.astype(BF)
        for n in range(HPG):
            outs[i, :, n * HD : (n + 1) * HD] = turned[n * W : (n + 1) * W]
        go(0, i)

    def gradients(i, step, e, values):
        factor = jnp.exp2((mb[i, step] - mcur[i]) * LOG2) * stat[i, 1:2, :]
        prob = e.astype(F32) * factor
        dscore = prob * (dot(values, dot_t[i]) - stat[i, 0:1, :])
        return prob.astype(BF), dscore.astype(BF)

    def backward_window(i):
        prob, dscore = gradients(i, 5, wb[i], vrb[i])
        dvrs[i] = dot(prob, natural(dob, i)).astype(BF)
        dkrs[i] = (dot(dscore, natural(qb, i)) * SCALE).astype(BF)
        dqacc[i] = dot(krb[i].T, dscore)
        go(2, i)
        go(3, i)

    def backward(i, step, first):
        grads, queries = natural(dob, i), natural(qb, i)
        total = dqacc[i]
        for a in chunks_of(step):
            prob, dscore = gradients(i, step, eb[i, a], kv[a, :, 1].reshape(CHUNK, HD))
            dv, dk = dot(prob, grads), dot(dscore, queries)
            dvacc[a] = dv if first else dvacc[a] + dv
            dkacc[a] = dk if first else dkacc[a] + dk
            total = total + dot(kt[a], dscore)
        dqacc[i] = total

    def finish_dq(i):
        turned = (dqacc[i] * SCALE).T.astype(BF)
        for n in range(HPG):
            dqs[i, :, n * HD : (n + 1) * HD] = turned[n * W : (n + 1) * W]
        go(1, i)

    def reach(kind, direction):
        return 4 if kind == direction else 3

    def scatter(kind, direction, hop, piece):
        return pltpu.make_async_remote_copy(
            src_ref=rs_s.at[direction, kind, hop - 1, piece],
            dst_ref=rs_r.at[direction, kind, hop - 1, piece],
            send_sem=rs_ss.at[direction, kind, hop - 1, piece],
            recv_sem=rs_rs.at[direction, kind, hop - 1, piece],
            device_id=ring(direction),
            device_id_type=MESH,
        )

    def partial(kind, a, piece):
        rows = slice(piece * PIECE, (piece + 1) * PIECE)
        return dkacc[a, rows] * SCALE if kind == 0 else dvacc[a, rows]

    def arrived(kind, direction, away, piece):
        hop = reach(kind, direction) - away
        scatter(kind, direction, hop, piece).wait_recv()
        return rs_r[direction, kind, hop - 1, piece].astype(F32)

    def pass_on(kind, direction, away, piece):
        total = partial(kind, away if direction == UP else (Y - away) % Y, piece)
        if away < reach(kind, direction):
            total = total + arrived(kind, direction, away, piece)
        hop = reach(kind, direction) - away + 1
        rs_s[direction, kind, hop - 1, piece] = total.astype(BF)
        scatter(kind, direction, hop, piece).start()

    def pass_all(away, piece):
        for kind, direction in ((0, UP), (1, DOWN), (1, UP), (0, DOWN)):
            if away <= reach(kind, direction):
                pass_on(kind, direction, away, piece)

    spread(0)
    ready(0)
    for i in (1, 2, 3):
        spread(i)
    turn(0)
    forward(0, 0)
    for i in range(X):
        hop_on(1, i)
    turn(1)
    turn(7)
    forward(0, 1)
    ready(1)
    forward(1, 0)
    forward(1, 1)
    ready(2)
    forward(2, 0)
    hop_on(2, 0)
    hop_on(2, 1)
    forward(2, 1)
    hop_on(2, 2)
    hop_on(2, 3)
    turn(2)
    turn(6)
    forward(0, 2)
    forward(1, 2)
    hop_on(3, 0)
    ready(3)
    forward(3, 0)
    hop_on(3, 1)
    forward(2, 2)
    hop_on(3, 2)
    forward(3, 1)
    hop_on(3, 3)
    turn(3)
    turn(5)
    forward(3, 2)
    forward(0, 3)
    forward(1, 3)
    for i in range(X):
        hop_on(4, i)
    turn(4)
    forward(2, 3)
    forward(3, 3)
    for i in range(X):
        forward(i, 4)
    order = (3, 2, 1, 0)
    for i in order:
        finish(i)
        backward_window(i)
    for n, i in enumerate(order):
        backward(i, 4, n == 0)
    for piece in range(PIECES):
        pass_all(4, piece)
    for n, i in enumerate(order):
        backward(i, 3, n == 0)
    for piece in range(PIECES):
        pass_all(3, piece)
    for n, i in enumerate(order):
        backward(i, 2, n == 0)
        pass
    for piece in range(PIECES):
        pass_all(2, piece)
    for n, i in enumerate(order):
        backward(i, 1, n == 0)
        backward(i, 0, n == 0)
        finish_dq(i)
    for piece in range(PIECES):
        pass_all(1, piece)
    for piece in range(PIECES):
        for kind in (0, 1):
            total = partial(kind, 0, piece) + arrived(kind, UP, 0, piece) + arrived(kind, DOWN, 0, piece)
            for n in range(PIECE // W):
                fin[kind, piece * (PIECE // W) + n] = total[n * W : (n + 1) * W].astype(BF)
                go(kind + 4, piece * (PIECE // W) + n)

    for kind in range(6):
        for d in (1, 2, 3):
            enter(kind, d).wait_send()
    for hop in range(1, 5):
        for direction in (UP, DOWN):
            for i in range(X):
                gather(hop, direction, i).wait_send()
    for kind in (0, 1):
        for direction in (UP, DOWN):
            for hop in range(1, reach(kind, direction) + 1):
                for piece in range(PIECES):
                    scatter(kind, direction, hop, piece).wait_send()
    for kind in range(6):
        leave_own(kind).wait()
        for d in (1, 2, 3):
            leave(kind, d).wait()


def hand_over(*refs):
    ins, outs, held, sems = refs[:6], refs[6:12], refs[12:18], refs[18]
    first = [pltpu.make_async_copy(ins[n], held[n], sems.at[0, n]) for n in range(6)]
    second = [pltpu.make_async_copy(held[n], outs[n], sems.at[1, n]) for n in range(6)]
    for copy in first:
        copy.start()
    for n in range(6):
        first[n].wait()
        second[n].start()
    for copy in second:
        copy.wait()


def body(q_resp, k_resp, v_resp, k_prompt, v_prompt, d_out, owner, lengths, visible):
    hbm = pl.BlockSpec(memory_space=pltpu.HBM)
    smem = pl.BlockSpec(memory_space=pltpu.SMEM)
    wide = jax.ShapeDtypeStruct((W, H * HD), BF)
    narrow = jax.ShapeDtypeStruct((W, G * HD), BF)
    shapes = (wide, wide, narrow, narrow, narrow, narrow)
    dma = pltpu.SemaphoreType.DMA
    results = pl.pallas_call(
        kernel,
        out_shape=shapes,
        in_specs=[smem] * 3 + [hbm] * 6,
        out_specs=(hbm,) * 6,
        scratch_shapes=[
            pltpu.SMEM((2, X), jnp.int32),
            pltpu.VMEM((X, W, GW), BF),
            pltpu.VMEM((X, W, GW), BF),
            pltpu.VMEM((X, W, HD), BF),
            pltpu.VMEM((X, W, HD), BF),
            pltpu.VMEM((Y, X, 2, W, HD), BF),
            pltpu.VMEM((Y, HD, CHUNK), BF),
            pltpu.VMEM((Y, HD + 16, CHUNK), BF),
            pltpu.VMEM((X, HD, ROWS), BF),
            pltpu.VMEM((X, HD, ROWS), BF),
            pltpu.VMEM((X, Y, CHUNK, ROWS), BF),
            pltpu.VMEM((X, W, ROWS), BF),
            pltpu.VMEM((X, 6, 1, ROWS), F32),
            pltpu.VMEM((X, 1, ROWS), F32),
            pltpu.VMEM((X, HD + 16, ROWS), F32),
            pltpu.VMEM((X, 8, ROWS), F32),
            pltpu.VMEM((X, HD, ROWS), F32),
            pltpu.VMEM((Y, CHUNK, HD), F32),
            pltpu.VMEM((Y, CHUNK, HD), F32),
            pltpu.VMEM((X, W, GW), BF),
            pltpu.VMEM((X, W, GW), BF),
            pltpu.VMEM((X, W, HD), BF),
            pltpu.VMEM((X, W, HD), BF),
            pltpu.VMEM((2, 2, 4, PIECES, PIECE, HD), BF),
            pltpu.VMEM((2, 2, 4, PIECES, PIECE, HD), BF),
            pltpu.VMEM((2, X, W, HD), BF),
            dma((6,)), dma((6, 3)), dma((6, 3)),
            dma((4, 2, X)), dma((4, 2, X)),
            dma((6,)), dma((6, 3)), dma((6, 3)),
            dma((2, 2, 4, PIECES)), dma((2, 2, 4, PIECES)),
        ],
        compiler_params=pltpu.CompilerParams(
            collective_id=0, has_side_effects=True, vmem_limit_bytes=56 * 2**20
        ),
    )(owner, lengths, visible, q_resp, k_resp, v_resp, k_prompt, v_prompt, d_out)
    return pl.pallas_call(
        hand_over,
        out_shape=shapes,
        in_specs=[hbm] * 6,
        out_specs=(hbm,) * 6,
        scratch_shapes=[pltpu.VMEM(shape.shape, BF) for shape in shapes] + [dma((2, 6))],
    )(*results)


def solution(mesh):
    rows = P(("grp", "ctx"), None)
    in_specs = (rows,) * 6 + (P("grp"),) * 3
    return jax.shard_map(
        body, mesh=mesh, in_specs=in_specs, out_specs=(rows,) * 6, check_vma=False
    )
```

time: 452 us -> 60.6 us (0.13)
  the two profiles are of different devices: /device:TPU:16 before, /device:TPU:2 now
where the time goes in v1:
time: 60.6 us; the launch traced here: 60.5 us
  Pallas kernels  59.7 us (99%)
  between operations  0.8 us (1%)
    pallas_call x1, Pallas kernels, body(): pl.pallas_call(kernel, out_shape=shapes, in_specs=[smem] * 3 + [hbm] * 6,...  57.5 us
    pallas_call x1, Pallas kernels, body(): pl.pallas_call(hand_over, out_shape=shapes, in_specs=[hbm] * 6, out_specs...  2.19 us

profile of v1, /device:TPU:2, one launch (start us, length us, event | category | flops | bytes accessed | tf_op | source)
XLA Modules:
  0.0 60.5 jit_solution(9730868295308324826)
XLA Ops:
  0.6 57.5 %shard_map.136 = (bf16[64,4096]{1,0:T(8,128)(2,1)}, bf16[64,4096]{1,0:T(8,128)(2,1)}, bf16[64,512]{1,0:T(8,128)(2,1)}, bf16[64,512]{1,0:T(8,128)(2,1)}, bf16[64,...) custom-call(s32[32]{0:T(128)} %owner.1, s32[32]{0:T(128)} %lengths.1, s32[32]{0:T(128)} %visible.1, bf16[64,4096]{1,0:T(8,128)(2,1)} %q.1, ...), custom_call_target="tpu_custom_call" | custom-call | tf_op jit(solution)/shard_map/pallas_call | solution.py:417
  58.1 2.2 %shard_map.137 = (bf16[64,4096]{1,0:T(8,128)(2,1)}, bf16[64,4096]{1,0:T(8,128)(2,1)}, bf16[64,512]{1,0:T(8,128)(2,1)}, bf16[64,512]{1,0:T(8,128)(2,1)}, bf16[64,...) custom-call(bf16[64,4096]{1,0:T(8,128)(2,1)} %get-tuple-element.12.refs_0_, bf16[64,4096]{1,0:T(8,128)(2,1)} %get-tuple-element.13.refs_1_, ...), custom_call_target="tpu_custom_call" | custom-call | tf_op jit(solution)/shard_map/pallas_call | solution.py:458

commit v2 on v1

v2 whole, which is shorter than its diff:
```python
import functools
import math

import jax
import jax.numpy as jnp
from jax import lax
from jax.experimental import pallas as pl
from jax.experimental.pallas import tpu as pltpu
from jax.sharding import PartitionSpec as P

H = 32
G = 4
HD = 128
HPG = H // G
GW = HPG * HD
X = 4
Y = 8
W = 64
ROWS = HPG * W
CHUNK = X * W
NEG = -1e30
SCALE = 1.0 / math.sqrt(HD)
LOG2 = SCALE * math.log2(math.e)
MESH = pl.DeviceIdType.MESH
BF = jnp.bfloat16
F32 = jnp.float32
UP, DOWN = 0, 1
PIECES = 4
PIECE = CHUNK // PIECES
OFF = (0, 1, 3, 2)
SLOT = (0, 1, 3, 2)


def dot(a, b):
    return lax.dot_general(a, b, (((1,), (0,)), ((), ())), preferred_element_type=F32)


def kernel(
    owner, lengths, visible, q, kr, vr, kp, vp, do,
    out, dq, dkp, dvp, dkr, dvr,
    slots, qb, dob, krb, vrb, kv, kt, vt, qt, dot_t, eb, wb, mb, mcur, oacc, stat,
    dqacc, dkacc, dvacc, outs, dqs, dkrs, dvrs, rs_s, rs_r, fin,
    in_ls, kv_ss, in_ss, in_rs, ag_ss, ag_rs, out_ls, out_ss, out_rs, rs_ss, rs_rs,
):
    c = lax.axis_index("ctx")
    y = c // X
    x = lax.rem(c, X)

    def at(rows, columns):
        return {"ctx": lax.rem(y + rows + Y, Y) * X + lax.rem(x + columns, X)}

    def drain(sem, kib):
        n = -(-kib // 256)
        while kib % n or kib // n % 16:
            n += 1
        ref = eb.at[0, 0:n, 0 : kib // n]
        pltpu.make_async_copy(ref, ref, sem).wait()

    def send(src, dst, send_sem, recv_sem, rows, columns):
        pltpu.make_async_remote_copy(
            src_ref=src,
            dst_ref=dst,
            send_sem=send_sem,
            recv_sem=recv_sem,
            device_id=at(rows, columns),
            device_id_type=MESH,
        ).start()

    partners = [(0, d) for d in (1, 2, 3)] + [(2, 0), (-2, 0)]
    partners += [(rows, d) for rows in (1, -1) for d in range(X)]
    barrier = pltpu.get_barrier_semaphore()
    for rows, columns in partners:
        pl.semaphore_signal(barrier, inc=1, device_id=at(rows, columns), device_id_type=MESH)

    sources = ((kp, HD), (vp, HD), (kr, HD), (vr, HD), (q, GW), (do, GW))

    def landing(kind, slot):
        if kind < 2:
            return kv.at[0, slot, kind]
        return (krb, vrb, qb, dob)[kind - 2].at[slot]

    parts = ((0, 1), (4,), (2, 3), (5,))
    part_kib = (32, 128, 32, 128)

    def enter(part, d, rows=0):
        slot = SLOT[-d % X]
        for kind in parts[part]:
            ref, width = sources[kind]
            column = pl.multiple_of(lax.rem(x + d, X) * width, HD)
            src = ref.at[:, pl.ds(column, width)]
            if part == 0:
                arrival = in_rs.at[0, slot - 1] if rows == 0 else ag_rs.at[0, slot]
                send(src, kv.at[-rows % Y, slot, kind], kv_ss, arrival, rows, d)
            else:
                send(src, landing(kind, slot), in_ss, in_rs.at[part, slot - 1], 0, d)

    def enter_own(part):
        for kind in parts[part]:
            ref, width = sources[kind]
            column = pl.multiple_of(x * width, HD)
            pltpu.make_async_copy(
                ref.at[:, pl.ds(column, width)], landing(kind, 0), in_ls.at[part]
            ).start()

    def entered(part, i):
        drain(in_ls.at[part] if i == 0 else in_rs.at[part, i - 1], part_kib[part])

    for part in range(4):
        enter_own(part)

    for i in range(X):
        holder = y * X + lax.rem(x + OFF[i], X)

        def count(j, carry, holder=holder):
            hit = owner[j] == holder
            return (
                carry[0] + jnp.where(hit, lengths[j], 0),
                carry[1] + jnp.where(hit, visible[j], 0),
            )

        length, seen = lax.fori_loop(0, Y * X, count, (jnp.int32(0), jnp.int32(0)))
        slots[0, i] = length
        slots[1, i] = seen

    pl.semaphore_wait(barrier, len(partners))
    for d in (0, 1, 3, 2):
        enter(0, d, 1)
        enter(0, d, -1)
        if d:
            enter(0, d)
    for part in (1, 2, 3):
        for d in (1, 3, 2):
            enter(part, d)

    def gather(hop, direction, i):
        sign = 1 if direction == UP else -1
        src, dst = -sign * (hop - 1) % Y, -sign * hop % Y
        if hop == 4:
            src = -sign * 2 % Y
            send(
                kv.at[src, i, direction], kv.at[4, i, direction],
                ag_ss, ag_rs.at[3, i], 2 * sign, 0,
            )
        else:
            send(kv.at[src, i], kv.at[dst, i], ag_ss, ag_rs.at[hop - 1, i], sign, 0)

    def hop_on(hop, i):
        drain(ag_rs.at[hop - 1, i], 64 if hop < 4 else 32)
        for after in {1: (2,), 2: (3, 4)}.get(hop, ()):
            gather(after, UP, i)
            gather(after, DOWN, i)

    def turn(a):
        kt[a] = kv[a, :, 0].reshape(CHUNK, HD).T
        vt[a, 0:HD, :] = kv[a, :, 1].reshape(CHUNK, HD).T
        vt[a, HD:, :] = jnp.ones((16, CHUNK), BF)

    def natural(ref, i):
        return jnp.concatenate([ref[i, :, n * HD : (n + 1) * HD] for n in range(HPG)], axis=0)

    def chunks_of(step):
        return (step,) if step in (0, 4) else (Y - step, step)

    def soften(i, step, scores, top, values_t, keep):
        if step != 0:
            before = mcur[i]
            top = jnp.maximum(top, before)
        mcur[i] = top
        mb[i, step] = top
        total = None
        for s, values, ref in zip(scores, values_t, keep):
            e = jnp.exp2((s - top) * LOG2).astype(BF)
            ref[...] = e
            term = dot(values, e)
            total = term if total is None else total + term
        if step == 0:
            oacc[i] = total
        else:
            oacc[i] = oacc[i] * jnp.exp2((before - top) * LOG2) + total

    def ready(i):
        entered(1, i)
        qt[i] = natural(qb, i).T

    def score(i, step):
        if step == 5:
            entered(2, i)
            key = lax.broadcasted_iota(jnp.int32, (W, ROWS), 0)
            query = lax.rem(lax.broadcasted_iota(jnp.int32, (W, ROWS), 1), W)
            allowed = (key >= W - slots[0, i]) & (key <= query)
            scores = [jnp.where(allowed, dot(krb[i], qt[i]), NEG)]
            values = [jnp.concatenate([vrb[i].T, jnp.ones((16, W), BF)], axis=0)]
            keep = [wb.at[i]]
        else:
            seen = slots[1, i]
            scores, values, keep = [], [], []
            for a in chunks_of(step):
                s = dot(kv[a, :, 0].reshape(CHUNK, HD), qt[i])
                first = lax.rem(y + a, Y) * CHUNK
                key = lax.broadcasted_iota(jnp.int32, (W, HD), 0) + first
                left = jnp.concatenate([key + lax.rem(x + OFF[n], X) * W for n in range(X)], axis=0)
                hide = jnp.where(left < seen, 0.0, NEG)
                scores.append(s + jnp.concatenate([hide] * (ROWS // HD), axis=1))
                values.append(vt[a])
                keep.append(eb.at[i, a])
        top = functools.reduce(
            jnp.maximum, [jnp.max(s, axis=0, keepdims=True) for s in scores]
        )
        return i, step, scores, top, values, keep

    def forward(*blocks):
        waiting = None
        for block in blocks:
            scored = score(*block)
            if waiting is not None:
                soften(*waiting)
            waiting = scored
        soften(*waiting)

    results = (
        (outs, out, GW), (dqs, dq, GW), (dkrs, dkr, HD), (dvrs, dvr, HD),
        (fin.at[0], dkp, HD), (fin.at[1], dvp, HD),
    )

    def go(kind, i):
        ref, target, width = results[kind]
        dst = target.at[:, pl.ds(pl.multiple_of(x * width, HD), width)]
        if i == 0:
            pltpu.make_async_copy(ref.at[0], dst, out_ls).start()
        else:
            send(ref.at[i], dst, out_ss, out_rs, 0, OFF[i])

    def finish(i):
        entered(3, i)
        inverse = 1.0 / oacc[i, HD : HD + 1, :]
        attended = oacc[i, 0:HD, :] * inverse
        grads_t = natural(dob, i).T
        dot_t[i] = grads_t
        stat[i, 0:1, :] = jnp.sum(grads_t.astype(F32) * attended, axis=0, keepdims=True)
        stat[i, 1:2, :] = inverse
        turned = attended.T.astype(BF)
        for n in range(HPG):
            outs[i, :, n * HD : (n + 1) * HD] = turned[n * W : (n + 1) * W]
        go(0, i)

    def gradients(i, step, e, values):
        factor = jnp.exp2((mb[i, step] - mcur[i]) * LOG2) * stat[i, 1:2, :]
        prob = e.astype(F32) * factor
        dscore = prob * (dot(values, dot_t[i]) - stat[i, 0:1, :])
        return prob.astype(BF), dscore.astype(BF)

    def backward_window(i):
        prob, dscore = gradients(i, 5, wb[i], vrb[i])
        dvrs[i] = dot(prob, natural(dob, i)).astype(BF)
        dkrs[i] = (dot(dscore, natural(qb, i)) * SCALE).astype(BF)
        dqacc[i] += dot(krb[i].T, dscore)
        go(2, i)
        go(3, i)

    def backward(i, step, first):
        grads, queries = natural(dob, i), natural(qb, i)
        total = 0.0 if step == 4 else dqacc[i]
        for a in chunks_of(step):
            prob, dscore = gradients(i, step, eb[i, a], kv[a, :, 1].reshape(CHUNK, HD))
            dv, dk = dot(prob, grads), dot(dscore, queries)
            dvacc[a] = dv if first else dvacc[a] + dv
            dkacc[a] = dk if first else dkacc[a] + dk
            total = total + dot(kt[a], dscore)
        dqacc[i] = total

    def finish_dq(i):
        turned = (dqacc[i] * SCALE).T.astype(BF)
        for n in range(HPG):
            dqs[i, :, n * HD : (n + 1) * HD] = turned[n * W : (n + 1) * W]
        go(1, i)

    def partial(kind, a, piece):
        rows = slice(piece * PIECE, (piece + 1) * PIECE)
        return dkacc[a, rows] * SCALE if kind == 0 else dvacc[a, rows]

    def pass_on(away, piece):
        if away == 4:
            for kind, sign in ((0, 1), (1, -1)):
                rs_s[3, kind, 0, piece] = partial(kind, 4, piece).astype(BF)
                send(
                    rs_s.at[3, kind, 0, piece], rs_r.at[3, kind, 0, piece],
                    rs_ss, rs_rs.at[0, piece], 2 * sign, 0,
                )
            return
        if away < 3:
            drain(rs_rs.at[2 - away, piece], (384 if away == 2 else 256) // PIECES)
        for kind in (0, 1):
            for direction in (UP, DOWN):
                sign = 1 if direction == UP else -1
                total = partial(kind, sign * away % Y, piece)
                if away < 3:
                    total = total + rs_r[away, kind, direction, piece].astype(F32)
                if away == 2 and kind == direction:
                    total = total + rs_r[3, kind, 0, piece].astype(F32)
                total = total.astype(BF)
                rs_s[away - 1, kind, direction, piece] = total
                send(
                    rs_s.at[away - 1, kind, direction, piece],
                    rs_r.at[away - 1, kind, direction, piece],
                    rs_ss, rs_rs.at[3 - away, piece], sign, 0,
                )

    def pass_out(piece):
        drain(rs_rs.at[2, piece], 256 // PIECES)
        for kind in (0, 1):
            total = partial(kind, 0, piece)
            for direction in (UP, DOWN):
                total = total + rs_r[0, kind, direction, piece].astype(F32)
            for n in range(PIECE // W):
                fin[kind, piece * (PIECE // W) + n] = total[n * W : (n + 1) * W].astype(BF)
                go(4 + kind, piece * (PIECE // W) + n)

    entered(0, 0)
    ready(0)
    hop_on(1, 0)
    entered(0, 1)
    entered(0, 2)
    hop_on(1, 1)
    hop_on(1, 2)
    entered(0, 3)
    hop_on(1, 3)
    turn(0)
    turn(1)
    turn(7)
    forward((0, 0), (0, 1))
    for i in range(X):
        hop_on(2, i)
    turn(2)
    turn(6)
    ready(1)
    forward((1, 0), (0, 2), (1, 1))
    ready(2)
    forward((2, 0), (1, 2), (2, 1), (2, 2))
    for i in range(X):
        hop_on(3, i)
    turn(3)
    turn(5)
    forward((0, 3), (1, 3), (2, 3))
    for i in range(X):
        hop_on(4, i)
    turn(4)
    ready(3)
    forward((3, 0), (0, 4), (3, 1), (1, 4), (3, 2), (2, 4), (3, 3), (3, 4))
    forward((0, 5), (1, 5), (2, 5), (3, 5))
    for i in range(X):
        finish(i)
        backward(i, 4, i == 0)
        if i == 3:
            for piece in range(PIECES):
                pass_on(4, piece)
        backward(i, 3, i == 0)
        if i == 3:
            for piece in range(PIECES):
                pass_on(3, piece)
    for i in (3, 2):
        backward_window(i)
        for step in (2, 1, 0):
            backward(i, step, i == 3)
        finish_dq(i)
    backward(1, 2, False)
    backward(0, 2, False)
    for piece in range(PIECES):
        pass_on(2, piece)
    backward_window(1)
    backward(1, 1, False)
    backward(1, 0, False)
    finish_dq(1)
    backward(0, 1, False)
    for piece in range(PIECES):
        pass_on(1, piece)
    backward_window(0)
    backward(0, 0, False)
    finish_dq(0)
    for piece in range(PIECES):
        pass_out(piece)

    drain(kv_ss, 352)
    drain(in_ss, 864)
    drain(ag_ss, 640)
    drain(rs_ss, 896)
    drain(out_ss, 960)
    drain(out_rs, 960)
    drain(out_ls, 320)


def hand_over(*refs):
    ins, outs, held, sems = refs[:6], refs[6:12], refs[12:18], refs[18]
    first = [pltpu.make_async_copy(ins[n], held[n], sems.at[0, n]) for n in range(6)]
    second = [pltpu.make_async_copy(held[n], outs[n], sems.at[1, n]) for n in range(6)]
    for copy in first:
        copy.start()
    for n in range(6):
        first[n].wait()
        second[n].start()
    for copy in second:
        copy.wait()


def body(q_resp, k_resp, v_resp, k_prompt, v_prompt, d_out, owner, lengths, visible):
    hbm = pl.BlockSpec(memory_space=pltpu.HBM)
    smem = pl.BlockSpec(memory_space=pltpu.SMEM)
    wide = jax.ShapeDtypeStruct((W, H * HD), BF)
    narrow = jax.ShapeDtypeStruct((W, G * HD), BF)
    shapes = (wide, wide, narrow, narrow, narrow, narrow)
    dma = pltpu.SemaphoreType.DMA
    results = pl.pallas_call(
        kernel,
        out_shape=shapes,
        in_specs=[smem] * 3 + [hbm] * 6,
        out_specs=(hbm,) * 6,
        scratch_shapes=[
            pltpu.SMEM((2, X), jnp.int32),
            pltpu.VMEM((X, W, GW), BF),
            pltpu.VMEM((X, W, GW), BF),
            pltpu.VMEM((X, W, HD), BF),
            pltpu.VMEM((X, W, HD), BF),
            pltpu.VMEM((Y, X, 2, W, HD), BF),
            pltpu.VMEM((Y, HD, CHUNK), BF),
            pltpu.VMEM((Y, HD + 16, CHUNK), BF),
            pltpu.VMEM((X, HD, ROWS), BF),
            pltpu.VMEM((X, HD, ROWS), BF),
            pltpu.VMEM((X, Y, CHUNK, ROWS), BF),
            pltpu.VMEM((X, W, ROWS), BF),
            pltpu.VMEM((X, 6, 1, ROWS), F32),
            pltpu.VMEM((X, 1, ROWS), F32),
            pltpu.VMEM((X, HD + 16, ROWS), F32),
            pltpu.VMEM((X, 8, ROWS), F32),
            pltpu.VMEM((X, HD, ROWS), F32),
            pltpu.VMEM((Y, CHUNK, HD), F32),
            pltpu.VMEM((Y, CHUNK, HD), F32),
            pltpu.VMEM((X, W, GW), BF),
            pltpu.VMEM((X, W, GW), BF),
            pltpu.VMEM((X, W, HD), BF),
            pltpu.VMEM((X, W, HD), BF),
            pltpu.VMEM((4, 2, 2, PIECES, PIECE, HD), BF),
            pltpu.VMEM((4, 2, 2, PIECES, PIECE, HD), BF),
            pltpu.VMEM((2, X, W, HD), BF),
            dma((4,)), dma, dma, dma((4, 3)),
            dma, dma((4, X)),
            dma, dma, dma,
            dma, dma((3, PIECES)),
        ],
        compiler_params=pltpu.CompilerParams(
            collective_id=0, has_side_effects=True, vmem_limit_bytes=56 * 2**20
        ),
    )(owner, lengths, visible, q_resp, k_resp, v_resp, k_prompt, v_prompt, d_out)
    return pl.pallas_call(
        hand_over,
        out_shape=shapes,
        in_specs=[hbm] * 6,
        out_specs=(hbm,) * 6,
        scratch_shapes=[pltpu.VMEM(shape.shape, BF) for shape in shapes] + [dma((2, 6))],
    )(*results)


def solution(mesh):
    rows = P(("grp", "ctx"), None)
    in_specs = (rows,) * 6 + (P("grp"),) * 3
    return jax.shard_map(
        body, mesh=mesh, in_specs=in_specs, out_specs=(rows,) * 6, check_vma=False
    )
```

time: 60.6 us -> 53.3 us (0.88)
  Pallas kernels: 59.7 us -> 52.4 us
    pallas_call x1, Pallas kernels: 57.5 us -> 50.2 us  [body(): pl.pallas_call(kernel, out_shape=shapes, in_specs=[smem] * 3 + [hbm] * 6,...]
where the time goes in v2:
time: 53.3 us; the launch traced here: 53.2 us
  Pallas kernels  52.4 us (98%)
  between operations  0.8 us (2%)
    pallas_call x1, Pallas kernels, body(): pl.pallas_call(kernel, out_shape=shapes, in_specs=[smem] * 3 + [hbm] * 6,...  50.2 us
    pallas_call x1, Pallas kernels, body(): pl.pallas_call(hand_over, out_shape=shapes, in_specs=[hbm] * 6, out_specs...  2.19 us

profile of v2, /device:TPU:2, one launch (start us, length us, event | category | flops | bytes accessed | tf_op | source)
XLA Modules:
  0.0 53.2 jit_solution(12105692985772361721)
XLA Ops:
  0.6 50.2 %shard_map.136 = (bf16[64,4096]{1,0:T(8,128)(2,1)}, bf16[64,4096]{1,0:T(8,128)(2,1)}, bf16[64,512]{1,0:T(8,128)(2,1)}, bf16[64,512]{1,0:T(8,128)(2,1)}, bf16[64,...) custom-call(s32[32]{0:T(128)} %owner.1, s32[32]{0:T(128)} %lengths.1, s32[32]{0:T(128)} %visible.1, bf16[64,4096]{1,0:T(8,128)(2,1)} %q.1, ...), custom_call_target="tpu_custom_call" | custom-call | tf_op jit(solution)/shard_map/pallas_call | solution.py:411
  50.8 2.2 %shard_map.137 = (bf16[64,4096]{1,0:T(8,128)(2,1)}, bf16[64,4096]{1,0:T(8,128)(2,1)}, bf16[64,512]{1,0:T(8,128)(2,1)}, bf16[64,512]{1,0:T(8,128)(2,1)}, bf16[64,...) custom-call(bf16[64,4096]{1,0:T(8,128)(2,1)} %get-tuple-element.12.refs_0_, bf16[64,4096]{1,0:T(8,128)(2,1)} %get-tuple-element.13.refs_1_, ...), custom_call_target="tpu_custom_call" | custom-call | tf_op jit(solution)/shard_map/pallas_call | solution.py:452

commit v3 on v2

--- a/solution.py
+++ b/solution.py
@@ -39,8 +39,8 @@
     owner, lengths, visible, q, kr, vr, kp, vp, do,
     out, dq, dkp, dvp, dkr, dvr,
     slots, qb, dob, krb, vrb, kv, kt, vt, qt, dot_t, eb, wb, mb, mcur, oacc, stat,
-    dqacc, dkacc, dvacc, outs, dqs, dkrs, dvrs, rs_s, rs_r, fin,
-    in_ls, kv_ss, in_ss, in_rs, ag_ss, ag_rs, out_ls, out_ss, out_rs, rs_ss, rs_rs,
+    dqacc, dkacc, dvacc, outs, dqs, dkrs, dvrs, rs_s, rs_r, tail_s, tail_r, fin,
+    in_ls, kv_ss, in_ss, in_rs, ag_ss, ag_rs, out_ls, out_ss, out_rs, rs_ss, rs_rs, tail_ss, tail_rs,
 ):
     c = lax.axis_index("ctx")
     y = c // X
@@ -217,10 +217,7 @@
             waiting = scored
         soften(*waiting)
 
-    results = (
-        (outs, out, GW), (dqs, dq, GW), (dkrs, dkr, HD), (dvrs, dvr, HD),
-        (fin.at[0], dkp, HD), (fin.at[1], dvp, HD),
-    )
+    results = ((outs, out, GW), (dqs, dq, GW), (dkrs, dkr, HD), (dvrs, dvr, HD))
 
     def go(kind, i):
         ref, target, width = results[kind]
@@ -283,7 +280,7 @@
             for kind, sign in ((0, 1), (1, -1)):
                 rs_s[3, kind, 0, piece] = partial(kind, 4, piece).astype(BF)
                 send(
-                    rs_s.at[3, kind, 0, piece], rs_r.at[3, kind, 0, piece],
+                    rs_s.at[3, kind, 0, piece], rs_r.at[2, kind, 0, piece],
                     rs_ss, rs_rs.at[0, piece], 2 * sign, 0,
                 )
             return
@@ -294,26 +291,29 @@
                 sign = 1 if direction == UP else -1
                 total = partial(kind, sign * away % Y, piece)
                 if away < 3:
-                    total = total + rs_r[away, kind, direction, piece].astype(F32)
+                    total = total + rs_r[away - 1, kind, direction, piece].astype(F32)
                 if away == 2 and kind == direction:
-                    total = total + rs_r[3, kind, 0, piece].astype(F32)
+                    total = total + rs_r[2, kind, 0, piece].astype(F32)
                 total = total.astype(BF)
+                if away == 1:
+                    leave_sum(kind, 1 + direction, piece, total)
+                    continue
                 rs_s[away - 1, kind, direction, piece] = total
                 send(
                     rs_s.at[away - 1, kind, direction, piece],
-                    rs_r.at[away - 1, kind, direction, piece],
+                    rs_r.at[away - 2, kind, direction, piece],
                     rs_ss, rs_rs.at[3 - away, piece], sign, 0,
                 )
 
-    def pass_out(piece):
-        drain(rs_rs.at[2, piece], 256 // PIECES)
-        for kind in (0, 1):
-            total = partial(kind, 0, piece)
-            for direction in (UP, DOWN):
-                total = total + rs_r[0, kind, direction, piece].astype(F32)
-            for n in range(PIECE // W):
-                fin[kind, piece * (PIECE // W) + n] = total[n * W : (n + 1) * W].astype(BF)
-                go(4 + kind, piece * (PIECE // W) + n)
+    def leave_sum(kind, way, piece, total):
+        for n in range(PIECE // W):
+            i = piece * (PIECE // W) + n
+            tail_s[way, kind, i] = total[n * W : (n + 1) * W]
+            if way > 0 or i > 0:
+                send(
+                    tail_s.at[way, kind, i], tail_r.at[way, kind, SLOT[-OFF[i] % X]],
+                    tail_ss, tail_rs, (0, 1, -1)[way], OFF[i],
+                )
 
     entered(0, 0)
     ready(0)
@@ -328,25 +328,28 @@
     turn(1)
     turn(7)
     forward((0, 0), (0, 1))
-    for i in range(X):
-        hop_on(2, i)
+    hop_on(2, 0)
+    ready(1)
+    forward((1, 0))
+    hop_on(2, 1)
+    hop_on(2, 2)
+    forward((1, 1))
+    hop_on(2, 3)
     turn(2)
     turn(6)
-    ready(1)
-    forward((1, 0), (0, 2), (1, 1))
     ready(2)
-    forward((2, 0), (1, 2), (2, 1), (2, 2))
+    forward((0, 2), (2, 0), (1, 2), (2, 1), (2, 2))
+    ready(3)
+    forward((3, 0), (3, 1), (3, 2), (0, 5), (1, 5), (2, 5), (3, 5))
     for i in range(X):
         hop_on(3, i)
     turn(3)
     turn(5)
-    forward((0, 3), (1, 3), (2, 3))
+    forward((0, 3), (1, 3), (2, 3), (3, 3))
     for i in range(X):
         hop_on(4, i)
     turn(4)
-    ready(3)
-    forward((3, 0), (0, 4), (3, 1), (1, 4), (3, 2), (2, 4), (3, 3), (3, 4))
-    forward((0, 5), (1, 5), (2, 5), (3, 5))
+    forward((0, 4), (1, 4), (2, 4), (3, 4))
     for i in range(X):
         finish(i)
         backward(i, 4, i == 0)
@@ -357,35 +360,47 @@
         if i == 3:
             for piece in range(PIECES):
                 pass_on(3, piece)
-    for i in (3, 2):
-        backward_window(i)
-        for step in (2, 1, 0):
-            backward(i, step, i == 3)
-        finish_dq(i)
-    backward(1, 2, False)
-    backward(0, 2, False)
+    for i in (3, 2, 1, 0):
+        backward(i, 2, i == 3)
+    backward_window(3)
+    backward(3, 1, True)
+    backward(3, 0, True)
+    finish_dq(3)
     for piece in range(PIECES):
         pass_on(2, piece)
-    backward_window(1)
-    backward(1, 1, False)
-    backward(1, 0, False)
-    finish_dq(1)
+        i = 2 - piece * 2 // PIECES
+        if piece % 2 == 0:
+            backward_window(i)
+            backward(i, 1, False)
+        else:
+            backward(i, 0, False)
+            finish_dq(i)
+    backward_window(0)
     backward(0, 1, False)
+    backward(0, 0, False)
+    for piece in range(PIECES):
+        for kind in (0, 1):
+            leave_sum(kind, 0, piece, partial(kind, 0, piece).astype(BF))
+    finish_dq(0)
     for piece in range(PIECES):
         pass_on(1, piece)
-    backward_window(0)
-    backward(0, 0, False)
-    finish_dq(0)
-    for piece in range(PIECES):
-        pass_out(piece)
+    drain(tail_rs, 352)
+    for kind, target in ((0, dkp), (1, dvp)):
+        for i in range(X):
+            own = tail_s[0, kind, 0] if i == 0 else tail_r[0, kind, i]
+            total = own.astype(F32) + tail_r[1, kind, i].astype(F32) + tail_r[2, kind, i].astype(F32)
+            fin[kind, i] = total.astype(BF)
+            column = pl.multiple_of(lax.rem(x + OFF[i], X) * HD, HD)
+            pltpu.make_async_copy(fin.at[kind, i], target.at[:, pl.ds(column, HD)], out_ls).start()
 
     drain(kv_ss, 352)
     drain(in_ss, 864)
     drain(ag_ss, 640)
-    drain(rs_ss, 896)
-    drain(out_ss, 960)
-    drain(out_rs, 960)
-    drain(out_ls, 320)
+    drain(rs_ss, 640)
+    drain(tail_ss, 352)
+    drain(out_ss, 864)
+    drain(out_rs, 864)
+    drain(out_ls, 416)
 
 
 def hand_over(*refs):
@@ -438,12 +453,15 @@
             pltpu.VMEM((X, W, HD), BF),
             pltpu.VMEM((X, W, HD), BF),
             pltpu.VMEM((4, 2, 2, PIECES, PIECE, HD), BF),
-            pltpu.VMEM((4, 2, 2, PIECES, PIECE, HD), BF),
+            pltpu.VMEM((3, 2, 2, PIECES, PIECE, HD), BF),
+            pltpu.VMEM((3, 2, X, W, HD), BF),
+            pltpu.VMEM((3, 2, X, W, HD), BF),
             pltpu.VMEM((2, X, W, HD), BF),
             dma((4,)), dma, dma, dma((4, 3)),
             dma, dma((4, X)),
             dma, dma, dma,
-            dma, dma((3, PIECES)),
+            dma, dma((2, PIECES)),
+            dma, dma,
         ],
         compiler_params=pltpu.CompilerParams(
             collective_id=0, has_side_effects=True, vmem_limit_bytes=56 * 2**20

time: 53.3 us -> 52.3 us (0.981)
  Pallas kernels: 52.4 us -> 51.3 us
    pallas_call x1, Pallas kernels: 50.2 us -> 49.1 us  [body(): pl.pallas_call(kernel, out_shape=shapes, in_specs=[smem] * 3 + [hbm] * 6,...]
where the time goes in v3:
time: 52.3 us; the launch traced here: 52.1 us
  Pallas kernels  51.3 us (98%)
  between operations  0.8 us (2%)
    pallas_call x1, Pallas kernels, body(): pl.pallas_call(kernel, out_shape=shapes, in_specs=[smem] * 3 + [hbm] * 6,...  49.1 us
    pallas_call x1, Pallas kernels, body(): pl.pallas_call(hand_over, out_shape=shapes, in_specs=[hbm] * 6, out_specs...  2.19 us

profile of v3, /device:TPU:2, one launch (start us, length us, event | category | flops | bytes accessed | tf_op | source)
XLA Modules:
  0.0 52.1 jit_solution(13137187227920440688)
XLA Ops:
  0.6 49.1 %shard_map.136 = (bf16[64,4096]{1,0:T(8,128)(2,1)}, bf16[64,4096]{1,0:T(8,128)(2,1)}, bf16[64,512]{1,0:T(8,128)(2,1)}, bf16[64,512]{1,0:T(8,128)(2,1)}, bf16[64,...) custom-call(s32[32]{0:T(128)} %owner.1, s32[32]{0:T(128)} %lengths.1, s32[32]{0:T(128)} %visible.1, bf16[64,4096]{1,0:T(8,128)(2,1)} %q.1, ...), custom_call_target="tpu_custom_call" | custom-call | tf_op jit(solution)/shard_map/pallas_call | solution.py:426
  49.8 2.2 %shard_map.137 = (bf16[64,4096]{1,0:T(8,128)(2,1)}, bf16[64,4096]{1,0:T(8,128)(2,1)}, bf16[64,512]{1,0:T(8,128)(2,1)}, bf16[64,512]{1,0:T(8,128)(2,1)}, bf16[64,...) custom-call(bf16[64,4096]{1,0:T(8,128)(2,1)} %get-tuple-element.12.refs_0_, bf16[64,4096]{1,0:T(8,128)(2,1)} %get-tuple-element.13.refs_1_, ...), custom_call_target="tpu_custom_call" | custom-call | tf_op jit(solution)/shard_map/pallas_call | solution.py:470

commit v4 on v3

--- a/solution.py
+++ b/solution.py
@@ -89,7 +89,7 @@
             column = pl.multiple_of(lax.rem(x + d, X) * width, HD)
             src = ref.at[:, pl.ds(column, width)]
             if part == 0:
-                arrival = in_rs.at[0, slot - 1] if rows == 0 else ag_rs.at[0, slot]
+                arrival = in_rs.at[0, slot - 1] if rows == 0 else ag_rs.at[0, slot, (1 - rows) // 2]
                 send(src, kv.at[-rows % Y, slot, kind], kv_ss, arrival, rows, d)
             else:
                 send(src, landing(kind, slot), in_ss, in_rs.at[part, slot - 1], 0, d)
@@ -139,16 +139,16 @@
             src = -sign * 2 % Y
             send(
                 kv.at[src, i, direction], kv.at[4, i, direction],
-                ag_ss, ag_rs.at[3, i], 2 * sign, 0,
+                ag_ss, ag_rs.at[3, i, direction], 2 * sign, 0,
             )
         else:
-            send(kv.at[src, i], kv.at[dst, i], ag_ss, ag_rs.at[hop - 1, i], sign, 0)
+            send(kv.at[src, i], kv.at[dst, i], ag_ss, ag_rs.at[hop - 1, i, direction], sign, 0)
 
     def hop_on(hop, i):
-        drain(ag_rs.at[hop - 1, i], 64 if hop < 4 else 32)
-        for after in {1: (2,), 2: (3, 4)}.get(hop, ()):
-            gather(after, UP, i)
-            gather(after, DOWN, i)
+        for direction in (UP, DOWN):
+            drain(ag_rs.at[hop - 1, i, direction], 32 if hop < 4 else 16)
+            for after in {1: (2,), 2: (3, 4)}.get(hop, ()):
+                gather(after, direction, i)
 
     def turn(a):
         kt[a] = kv[a, :, 0].reshape(CHUNK, HD).T
@@ -281,13 +281,13 @@
                 rs_s[3, kind, 0, piece] = partial(kind, 4, piece).astype(BF)
                 send(
                     rs_s.at[3, kind, 0, piece], rs_r.at[2, kind, 0, piece],
-                    rs_ss, rs_rs.at[0, piece], 2 * sign, 0,
+                    rs_ss, rs_rs.at[0, piece, kind], 2 * sign, 0,
                 )
             return
-        if away < 3:
-            drain(rs_rs.at[2 - away, piece], (384 if away == 2 else 256) // PIECES)
-        for kind in (0, 1):
-            for direction in (UP, DOWN):
+        for direction in (UP, DOWN):
+            if away < 3:
+                drain(rs_rs.at[2 - away, piece, direction], (192 if away == 2 else 128) // PIECES)
+            for kind in (0, 1):
                 sign = 1 if direction == UP else -1
                 total = partial(kind, sign * away % Y, piece)
                 if away < 3:
@@ -302,7 +302,7 @@
                 send(
                     rs_s.at[away - 1, kind, direction, piece],
                     rs_r.at[away - 2, kind, direction, piece],
-                    rs_ss, rs_rs.at[3 - away, piece], sign, 0,
+                    rs_ss, rs_rs.at[3 - away, piece, direction], sign, 0,
                 )
 
     def leave_sum(kind, way, piece, total):
@@ -458,9 +458,9 @@
             pltpu.VMEM((3, 2, X, W, HD), BF),
             pltpu.VMEM((2, X, W, HD), BF),
             dma((4,)), dma, dma, dma((4, 3)),
-            dma, dma((4, X)),
+            dma, dma((4, X, 2)),
             dma, dma, dma,
-            dma, dma((2, PIECES)),
+            dma, dma((2, PIECES, 2)),
             dma, dma,
         ],
         compiler_params=pltpu.CompilerParams(

time: 52.3 us -> 52.1 us (level)
  the two profiles are of different devices: /device:TPU:2 before, /device:TPU:384 now
where the time goes in v4:
time: 52.1 us; the launch traced here: 52 us
  Pallas kernels  51.2 us (98%)
  between operations  0.8 us (2%)
    pallas_call x1, Pallas kernels, body(): pl.pallas_call(kernel, out_shape=shapes, in_specs=[smem] * 3 + [hbm] * 6,...  49 us
    pallas_call x1, Pallas kernels, body(): pl.pallas_call(hand_over, out_shape=shapes, in_specs=[hbm] * 6, out_specs...  2.19 us

profile of v4, /device:TPU:384, one launch (start us, length us, event | category | flops | bytes accessed | tf_op | source)
XLA Modules:
  0.0 52.0 jit_solution(694293078223813694)
XLA Ops:
  0.6 49.0 %shard_map.136 = (bf16[64,4096]{1,0:T(8,128)(2,1)}, bf16[64,4096]{1,0:T(8,128)(2,1)}, bf16[64,512]{1,0:T(8,128)(2,1)}, bf16[64,512]{1,0:T(8,128)(2,1)}, bf16[64,...) custom-call(s32[32]{0:T(128)} %owner.1, s32[32]{0:T(128)} %lengths.1, s32[32]{0:T(128)} %visible.1, bf16[64,4096]{1,0:T(8,128)(2,1)} %q.1, ...), custom_call_target="tpu_custom_call" | custom-call | tf_op jit(solution)/shard_map/pallas_call | solution.py:426
  49.6 2.2 %shard_map.137 = (bf16[64,4096]{1,0:T(8,128)(2,1)}, bf16[64,4096]{1,0:T(8,128)(2,1)}, bf16[64,512]{1,0:T(8,128)(2,1)}, bf16[64,512]{1,0:T(8,128)(2,1)}, bf16[64,...) custom-call(bf16[64,4096]{1,0:T(8,128)(2,1)} %get-tuple-element.12.refs_0_, bf16[64,4096]{1,0:T(8,128)(2,1)} %get-tuple-element.13.refs_1_, ...), custom_call_target="tpu_custom_call" | custom-call | tf_op jit(solution)/shard_map/pallas_call | solution.py:470
